TPU v7x, 128 devices: a whole 4x4x4 slice. The times are simulated.
128 devices in a mesh: leaf: 4 (over x), grid: 32 (over z, y, core).
Axes of the slice: x: 4, y: 4, z: 4, core: 2. Of those that a mesh axis runs over, the one named last changes fastest.
Arguments:
- rhs: bfloat16 [4, 1024, 1024], P('leaf', 'grid'), may hold values from -6 to 6
- inverse_blocks: bfloat16 [4, 1024, 1024], P('leaf'), as said below
- update_blocks: bfloat16 [4, 8, 1024, 1024], P('leaf', None, 'grid'), may hold values from -0.046875 to 0.046875
- targets: int32 [4, 8, 32], P('leaf', None, 'grid'), may hold values from -1 to 3, as said below
- widths: int32 [4], P('leaf'), may hold values from 128 to 1024, as said below
Outputs:
- forward: bfloat16 [4, 1024, 1024], P('leaf', 'grid')
- solution: bfloat16 [4, 1024, 1024], P('leaf', 'grid')
Inputs may be any that keep to these rules, and one draw needn't show every extreme that they name: `targets`: for supernode s every entry is -1 or a later supernode, greater than s; slot 0 is never -1 below the last supernode, all of whose entries are -1. `widths`: each is a multiple of 128; the last supernode's is 1024. `inverse_blocks`: each is lower triangular with a diagonal of positive entries.
All inputs are finite; a program needn't handle non-finite values.
Results may differ from a plain program's by a relative error of at most 0.0067.
Values may be sent and summed in bfloat16 or wider, within the bound.
A program may use at most 128 MiB of HBM per device.

v0:
```python
import jax
import jax.numpy as jnp
from jax import lax
from jax.sharding import PartitionSpec as P


def from_behind(value, axis, steps):
    count = lax.axis_size(axis)
    first, last = (max(0, -steps), min(count, count - steps))
    return lax.ppermute(value, axis, [(source, source + steps) for source in range(first, last)])


def local(rhs, inverse_blocks, update_blocks, targets, widths):
    node_count, piece_rows, columns = rhs.shape
    slot_count = update_blocks.shape[1]
    width_full = inverse_blocks.shape[2]
    leaves = lax.axis_size("leaf")
    total_nodes = node_count * leaves
    leaf_index = lax.axis_index("leaf")
    grid_index = lax.axis_index("grid")
    block_count = 1
    block_width = columns // block_count
    rounds = leaves + block_count - 1
    zero_index = jnp.int32(0)
    first_row = grid_index * piece_rows
    row_index = first_row + jnp.arange(piece_rows, dtype=jnp.int32)
    row_full = jnp.arange(width_full, dtype=jnp.int32)
    node_range = jnp.arange(total_nodes, dtype=jnp.int32)
    live_rows = [(row_index < widths[0])[:, None]]
    live_full = [(row_full < widths[0])[:, None]]
    routes = [(targets[0, :, 0][:, None] == node_range[None, :]).astype(jnp.float32)]
    flat_blocks = [update_blocks[0].reshape(slot_count * piece_rows, width_full)]
    forward = jnp.zeros((node_count, piece_rows, columns), jnp.bfloat16)
    forward_whole = jnp.zeros((node_count, width_full, columns), jnp.bfloat16)
    pending = jnp.zeros((total_nodes, piece_rows, block_width), jnp.float32)
    for round_id in range(rounds):
        offset = round_id - leaf_index
        active = (offset >= 0) & (offset < block_count)
        member = 0
        node_id = leaf_index * node_count + member
        source = rhs[member].astype(jnp.float32)
        waiting = lax.dynamic_index_in_dim(pending, node_id, 0, keepdims=False)
        corrected = jnp.where(live_rows[member], source - waiting, 0.0).astype(jnp.bfloat16)
        inverse_rows = inverse_blocks[member]
        blocks_here = flat_blocks[member]
        solved_all = jnp.dot(
            inverse_rows,
            lax.all_gather(corrected, "grid", axis=0, tiled=True),
            preferred_element_type=jnp.float32,
        )
        solved_all = jnp.where(live_full[member], solved_all, 0.0).astype(jnp.bfloat16)
        solved = lax.dynamic_slice_in_dim(solved_all, first_row, piece_rows, 0)
        products = jnp.dot(blocks_here, solved_all, preferred_element_type=jnp.float32)
        products = products.reshape(slot_count, piece_rows, block_width)
        pending = pending + jnp.einsum(
            "us,urk->srk", routes[member], products, precision=lax.Precision.HIGHEST
        )
        stored = solved[None]
        forward = jnp.where(active, stored, forward)
        stored_whole = solved_all[None]
        forward_whole = jnp.where(active, stored_whole, forward_whole)
        if round_id + 1 < rounds:
            pending = from_behind(pending, "leaf", 1)
    solution = jnp.zeros((node_count, piece_rows, columns), jnp.bfloat16)
    known = jnp.zeros((total_nodes, piece_rows, block_width), jnp.bfloat16)
    for round_id in range(rounds):
        offset = round_id - (leaves - 1 - leaf_index)
        active = (offset >= 0) & (offset < block_count)
        for member in reversed(range(node_count)):
            node_id = leaf_index * node_count + member
            inverse_rows = inverse_blocks[member]
            blocks_here = flat_blocks[member]
            gathered = jnp.einsum(
                "us,srk->urk",
                routes[member],
                known.astype(jnp.float32),
                precision=lax.Precision.HIGHEST,
            )
            gathered = gathered.astype(jnp.bfloat16).reshape(slot_count * piece_rows, block_width)
            local_term = lax.dot_general(
                blocks_here, gathered, (((0,), (0,)), ((), ())), preferred_element_type=jnp.float32
            )
            coupled = lax.psum(local_term, "grid")
            earlier = forward_whole[member].astype(jnp.float32)
            weighted = jnp.where(live_full[member], earlier - coupled, 0.0).astype(jnp.bfloat16)
            result_all = lax.dot_general(
                inverse_rows, weighted, (((0,), (0,)), ((), ())), preferred_element_type=jnp.float32
            )
            result_all = jnp.where(live_full[member], result_all, 0.0).astype(jnp.bfloat16)
            result = lax.dynamic_slice_in_dim(result_all, first_row, piece_rows, 0)
            known = lax.dynamic_update_slice(known, result[None], (node_id, zero_index, zero_index))
            stored = result[None]
            solution = jnp.where(active, stored, solution)
        if round_id + 1 < rounds:
            known = from_behind(known, "leaf", -1)
    return (forward, solution)


def solution(mesh):
    placed = (
        P("leaf", "grid", None),
        P("leaf", None, None),
        P("leaf", None, "grid", None),
        P("leaf", None, "grid"),
        P("leaf"),
    )
    return jax.shard_map(
        local,
        mesh=mesh,
        in_specs=placed,
        out_specs=(P("leaf", "grid", None), P("leaf", "grid", None)),
        check_vma=False,
    )
```

profile of v0, /device:TPU:1, one launch (start us, length us, event | category | flops | bytes accessed | tf_op | source)
XLA Modules:
  0.0 787.6 jit_solution(11807453150781167677)
XLA Ops:
  8.0 1.5 fusion.55
  9.7 48.8 %all-gather.5.cloned.1.call-done = bf16[1024,1024]{1,0:T(8,128)(2,1)} async-done(((bf16[32,1024]{1,0:T(8,128)(2,1)}), bf16[1024,1024]{1,0:T(8,128)(2,1)}) %all-gather.5.cloned.1.call-update) | async-done | bytes 2097168 | tf_op jit(solution)/shard_map/all_gather | solution.py:48
  58.5 3.9 select_convert_fusion.3
  63.2 2.0 fusion.46
  65.2 3.1 collective-permute-start
  68.3 11.3 %collective-permute-done = f32[4,32,1024]{2,0,1:T(4,128)S(1)} collective-permute-done((f32[4,32,1024]{2,0,1:T(4,128)}, f32[4,32,1024]{2,0,1:T(4,128)S(1)}, u32[]{:S(2)}, u32[]{:S(2)}) %collective-permute-start) | collective-permute-done | bytes 524320 | tf_op jit(solution)/shard_map/ppermute | solution.py:10
  80.6 45.1 %all-gather.7.cloned.1.call-done = bf16[1024,1024]{1,0:T(8,128)(2,1)} async-done(((bf16[32,1024]{1,0:T(8,128)(2,1)}), bf16[1024,1024]{1,0:T(8,128)(2,1)}) %all-gather.7.cloned.1.call-update) | async-done | bytes 2097168 | tf_op jit(solution)/shard_map/all_gather | solution.py:48
  125.7 4.0 select_convert_fusion.2
  131.0 1.2 convolution_add_fusion.1
  132.2 3.1 collective-permute-start.1
  135.3 11.0 %collective-permute-done.1 = f32[4,32,1024]{2,0,1:T(4,128)S(1)} collective-permute-done((f32[4,32,1024]{2,0,1:T(4,128)S(1)}, f32[4,32,1024]{2,0,1:T(4,128)S(1)}, u32[]{:S(2)}, u32[]{:S(2)}) %collective-permute-start.1) | collective-permute-done | bytes 524320 | tf_op jit(solution)/shard_map/ppermute | solution.py:10
  147.4 45.0 %all-gather.9.cloned.1.call-done = bf16[1024,1024]{1,0:T(8,128)(2,1)} async-done(((bf16[32,1024]{1,0:T(8,128)(2,1)}), bf16[1024,1024]{1,0:T(8,128)(2,1)}) %all-gather.9.cloned.1.call-update) | async-done | bytes 2097168 | tf_op jit(solution)/shard_map/all_gather | solution.py:48
  192.4 4.0 select_convert_fusion.1
  197.7 1.2 convolution_add_fusion
  198.9 3.1 collective-permute-start.2
  202.0 11.0 %collective-permute-done.2 = f32[4,32,1024]{2,0,1:T(4,128)S(1)} collective-permute-done((f32[4,32,1024]{2,0,1:T(4,128)S(1)}, f32[4,32,1024]{2,0,1:T(4,128)S(1)}, u32[]{:S(2)}, u32[]{:S(2)}) %collective-permute-start.2) | collective-permute-done | bytes 524320 | tf_op jit(solution)/shard_map/ppermute | solution.py:10
  214.6 2.8 convolution_bitcast_fusion.3
  217.8 3.9 copy.37
  221.8 3.9 copy.38
  225.7 33.5 %all-gather.11.cloned.1.call-done = bf16[1024,1024]{1,0:T(8,128)(2,1)} async-done(((bf16[32,1024]{1,0:T(8,128)(2,1)}), bf16[1024,1024]{1,0:T(8,128)(2,1)}) %all-gather.11.cloned.1.call-update) | async-done | bytes 2097168 | tf_op jit(solution)/shard_map/all_gather | solution.py:48
  259.1 5.3 select_convert_fusion
  264.4 4.0 copy.39
  268.4 3.7 select_select_fusion
  272.1 100.9 %all-reduce.5.cloned.1.call-done = f32[1024,1024]{1,0:T(8,128)} async-done(((f32[1024,1024]{1,0:T(8,128)}), f32[1024,1024]{1,0:T(8,128)}) %all-reduce.5.cloned.1.call-update) | async-done | bytes 4194320 | tf_op jit(solution)/shard_map/psum | solution.py:83
  373.0 5.6 fusion.14
  378.6 1.3 copy-done.6
  380.3 0.9 dynamic_update_slice.9
  381.2 1.3 collective-permute-start.3
  382.5 7.8 collective-permute-done.3
  391.0 2.8 convolution_bitcast_fusion.2
  393.8 112.5 %all-reduce.7.cloned.1.call-done = f32[1024,1024]{1,0:T(8,128)} async-done(((f32[1024,1024]{1,0:T(8,128)}), f32[1024,1024]{1,0:T(8,128)}) %all-reduce.7.cloned.1.call-update) | async-done | bytes 4194320 | tf_op jit(solution)/shard_map/psum | solution.py:83
  506.3 5.6 fusion.12
  511.9 1.3 copy-done.7
  513.6 0.9 dynamic_update_slice.10
  514.5 1.6 collective-permute-start.4
  516.0 7.5 collective-permute-done.4
  524.2 2.8 convolution_bitcast_fusion.1
  527.0 112.5 %all-reduce.9.cloned.1.call-done = f32[1024,1024]{1,0:T(8,128)} async-done(((f32[1024,1024]{1,0:T(8,128)}), f32[1024,1024]{1,0:T(8,128)}) %all-reduce.9.cloned.1.call-update) | async-done | bytes 4194320 | tf_op jit(solution)/shard_map/psum | solution.py:83
  639.6 5.6 fusion.10
  645.1 1.3 copy-done.8
  646.8 0.9 dynamic_update_slice.11
  647.7 1.3 collective-permute-start.5
  649.0 7.7 collective-permute-done.5
  657.4 2.8 convolution_bitcast_fusion
  661.3 1.4 select_bitcast_fusion
  663.5 109.4 %all-reduce.11.cloned.1.call-done = f32[1024,1024]{1,0:T(8,128)} async-done(((f32[1024,1024]{1,0:T(8,128)}), f32[1024,1024]{1,0:T(8,128)}) %all-reduce.11.cloned.1.call-update) | async-done | bytes 4194320 | tf_op jit(solution)/shard_map/psum | solution.py:83
  772.9 5.6 fusion.8
  778.4 1.5 fusion.54
  (64 shorter events, 13.1 us)
Async XLA Ops:
  7.2 51.4 %copy-start = (bf16[1,1024,1024]{2,1,0:T(8,128)(2,1)S(1)}, bf16[1,1024,1024]{2,1,0:T(8,128)(2,1)}, u32[]{:S(2)}) copy-start(bf16[1,1024,1024]{2,1,0:T(8,128)(2,1)} %param.6) | copy-start | bytes 6291460
  7.2 51.3 %all-gather.5.cloned.1.call-start = ((), (), s32[]{:S(2)}) async-start(), calls=%async_computation | async-start | bytes 2162688 | tf_op jit(solution)/shard_map/all_gather | solution.py:48
  9.6 116.1 %all-gather.7.cloned.1.call-start = ((), (), s32[]{:S(2)}) async-start(), calls=%async_computation.1 | async-start | bytes 2162688 | tf_op jit(solution)/shard_map/all_gather | solution.py:48
  9.7 52.8 %copy-start.1 = (bf16[1,8,32,1024]{3,2,1,0:T(8,128)(2,1)S(1)}, bf16[1,8,32,1024]{3,2,1,0:T(8,128)(2,1)}, u32[]{:S(2)}) copy-start(bf16[1,8,32,1024]{3,2,1,0:T(8,128)(2,1)} %param.7) | copy-start | bytes 1572868
  62.4 2.8 copy-start.4
  62.5 0.8 copy-start.9
  62.5 17.3 %copy-start.5 = (bf16[1,32,1024]{2,1,0:T(8,128)(2,1)S(1)}, bf16[1,32,1024]{2,1,0:T(8,128)(2,1)}, u32[]{:S(2)}) copy-start(bf16[1,32,1024]{2,1,0:T(8,128)(2,1)} %param.5) | copy-start | bytes 196612
  65.2 14.5 %collective-permute-start = (f32[4,32,1024]{2,0,1:T(4,128)}, f32[4,32,1024]{2,0,1:T(4,128)S(1)}, u32[]{:S(2)}, u32[]{:S(2)}) collective-permute-start(f32[4,32,1024]{2,0,1:T(4,128)} %fusion.46), channel_id=1, source_target_pairs={{0,32},{32,64},{64,96},{1,33},{33,65},{65,97},{2,34},{34,66},{66,9... | collective-permute-start | bytes 1572872 | tf_op jit(solution)/shard_map/ppermute | solution.py:10
  80.5 111.9 %all-gather.9.cloned.1.call-start = ((), (), s32[]{:S(2)}) async-start(), calls=%async_computation.2 | async-start | bytes 2162688 | tf_op jit(solution)/shard_map/all_gather | solution.py:48
  129.6 1.3 copy-start.2
  132.2 14.2 %collective-permute-start.1 = (f32[4,32,1024]{2,0,1:T(4,128)S(1)}, f32[4,32,1024]{2,0,1:T(4,128)S(1)}, u32[]{:S(2)}, u32[]{:S(2)}) collective-permute-start(f32[4,32,1024]{2,0,1:T(4,128)S(1)} %convolution_add_fusion.1), channel_id=1, source_target_pairs={{0,32},{32,64},{64,96},{1,33},{33,65},{65,97},{2,34},{34,66},{66,9... | collective-permute-start | bytes 1572872 | tf_op jit(solution)/shard_map/ppermute | solution.py:10
  147.2 111.9 %all-gather.11.cloned.1.call-start = ((), (), s32[]{:S(2)}) async-start(), calls=%async_computation.3 | async-start | bytes 2162688 | tf_op jit(solution)/shard_map/all_gather | solution.py:48
  196.4 1.3 copy-start.3
  198.9 14.2 %collective-permute-start.2 = (f32[4,32,1024]{2,0,1:T(4,128)S(1)}, f32[4,32,1024]{2,0,1:T(4,128)S(1)}, u32[]{:S(2)}, u32[]{:S(2)}) collective-permute-start(f32[4,32,1024]{2,0,1:T(4,128)S(1)} %convolution_add_fusion), channel_id=1, source_target_pairs={{0,32},{32,64},{64,96},{1,33},{33,65},{65,97},{2,34},{34,66},{66,9... | collective-permute-start | bytes 1572872 | tf_op jit(solution)/shard_map/ppermute | solution.py:10
  213.9 159.1 %all-reduce.5.cloned.1.call-start = ((), (), s32[]{:S(2)}) async-start(), calls=%async_computation.4 | async-start | bytes 8388608 | tf_op jit(solution)/shard_map/psum | solution.py:83
  217.5 288.9 %all-reduce.7.cloned.1.call-start = ((), (), s32[]{:S(2)}) async-start(), calls=%async_computation.5 | async-start | bytes 8388608 | tf_op jit(solution)/shard_map/psum | solution.py:83
  378.6 1.3 copy-start.6
  381.2 9.1 %collective-permute-start.3 = (bf16[4,32,1024]{2,0,1:T(4,128)(2,1)S(1)}, bf16[4,32,1024]{2,0,1:T(4,128)(2,1)S(1)}, u32[]{:S(2)}, u32[]{:S(2)}) collective-permute-start(bf16[4,32,1024]{2,0,1:T(4,128)(2,1)S(1)} %dynamic_update_slice.9), channel_id=1, source_target_pairs={{32,0},{64,32},{96,64},{33,1},{65,33},{97,65},{34,2},{66,34},{98,6... | collective-permute-start | bytes 786440 | tf_op jit(solution)/shard_map/ppermute | solution.py:10
  393.8 245.8 %all-reduce.9.cloned.1.call-start = ((), (), s32[]{:S(2)}) async-start(), calls=%async_computation.6 | async-start | bytes 8388608 | tf_op jit(solution)/shard_map/psum | solution.py:83
  511.9 1.3 copy-start.7
  514.5 9.0 %collective-permute-start.4 = (bf16[4,32,1024]{2,0,1:T(4,128)(2,1)S(1)}, bf16[4,32,1024]{2,0,1:T(4,128)(2,1)S(1)}, u32[]{:S(2)}, u32[]{:S(2)}) collective-permute-start(bf16[4,32,1024]{2,0,1:T(4,128)(2,1)S(1)} %dynamic_update_slice.10), channel_id=1, source_target_pairs={{32,0},{64,32},{96,64},{33,1},{65,33},{97,65},{34,2},{66,34},{98,6... | collective-permute-start | bytes 786440 | tf_op jit(solution)/shard_map/ppermute | solution.py:10
  527.0 245.9 %all-reduce.11.cloned.1.call-start = ((), (), s32[]{:S(2)}) async-start(), calls=%async_computation.7 | async-start | bytes 8388608 | tf_op jit(solution)/shard_map/psum | solution.py:83
  645.1 1.4 copy-start.8
  647.7 9.0 %collective-permute-start.5 = (bf16[4,32,1024]{2,0,1:T(4,128)(2,1)S(1)}, bf16[4,32,1024]{2,0,1:T(4,128)(2,1)S(1)}, u32[]{:S(2)}, u32[]{:S(2)}) collective-permute-start(bf16[4,32,1024]{2,0,1:T(4,128)(2,1)S(1)} %dynamic_update_slice.11), channel_id=1, source_target_pairs={{32,0},{64,32},{96,64},{33,1},{65,33},{97,65},{34,2},{66,34},{98,6... | collective-permute-start | bytes 786440 | tf_op jit(solution)/shard_map/ppermute | solution.py:10
Sparse Core Ops, SparseCore 0:
  10.9 47.6 all-gather.4
  80.7 44.9 all-gather.6
  147.3 45.0 all-gather.8
  214.0 45.0 all-gather.10
  262.3 110.6 all-reduce.4
  393.9 112.3 all-reduce.6
  527.1 112.3 all-reduce.8
  660.4 112.4 all-reduce.10
where the time goes:
time: 788 us
  waiting for transfers between devices  664 us (84%)
  matrix products  58.5 us (7%)
  local copies, waits for them, and re-layouts  24.6 us (3%)
  between operations  15.4 us (2%)
  starting transfers between devices  14.2 us (2%)
  other arithmetic  10.8 us (1%)
    psum x4, waiting for transfers between devices, local(): coupled = lax.psum(local_term, 'grid')  435 us
    all_gather x4, waiting for transfers between devices, local(): lax.all_gather(corrected, 'grid', axis=0, tiled=True)  172 us
    ppermute x6, waiting for transfers between devices, from_behind(): lax.ppermute(value, axis, [(source, source + steps) for source in range(f...  56.3 us
    dot_general x4, matrix products, local(): lax.dot_general(inverse_rows, weighted, (((0,), (0,)), ((), ())), preferr...  22.2 us
    dot_general x4, matrix products, local(): jnp.dot(inverse_rows, lax.all_gather(corrected, 'grid', axis=0, tiled=Tru...  17.1 us
  transfers between devices with their start and end apart: 14, of which 14 were waited for; matrix products, arithmetic and copies ran while one was open for 4% of the time, Pallas kernels for 0%

commit v1 on v0

v1 whole, which is shorter than its diff:
```python
import jax
import jax.numpy as jnp
from jax import lax
from jax.experimental import pallas as pl
from jax.experimental.pallas import tpu as pltpu
from jax.sharding import PartitionSpec as P

MESH = pl.DeviceIdType.MESH
W = 1024
PIECE = 32
GRID = 32
LINE = 4
SLOTS = 8
HALF = W // 2
NEAR = (0, -1, 1, 2)
F32 = jnp.float32
BF16 = jnp.bfloat16


def product(a, b, transposed=False):
    dims = (((1,), (1 if transposed else 0,)), ((), ()))
    return lax.dot_general(a, b, dims, preferred_element_type=F32)


def kernel(
    rhs_h, inv_h, upd_h, tgt_s, wid_s, fwd_o, sol_o,
    rhs_v, inv_v, upd_v, mats, rbuf, fbuf, obuf, wide, fsend, osend,
    part_out, part_in, state,
    in_sem, gat_send, gat_recv, all_send, all_recv, hop_send, hop_recv,
):
    leaf = lax.axis_index("leaf")
    g = lax.axis_index("grid")
    z, y, c = g // 8, (g // 2) % LINE, g % 2
    place = (z, y)

    def device(x, zz, yy, cc):
        return (x, ((zz % LINE) * LINE + (yy % LINE)) * 2 + cc)

    loads = [
        pltpu.make_async_copy(upd_h, upd_v, in_sem.at[0]),
        pltpu.make_async_copy(inv_h, inv_v, in_sem.at[1]),
        pltpu.make_async_copy(rhs_h, rhs_v, in_sem.at[2]),
    ]
    for load in loads:
        load.start()

    barrier = pltpu.get_barrier_semaphore()

    def greet(d, carry):
        pl.semaphore_signal(barrier, inc=1, device_id=(leaf, (g + d) % GRID), device_id_type=MESH)
        return carry

    lax.fori_loop(1, GRID, greet, 0)
    for d in (1, 2, 3):
        pl.semaphore_signal(barrier, inc=1, device_id=((leaf + d) % 4, g), device_id_type=MESH)

    width = wid_s[0]

    def live(rows):
        return lax.broadcasted_iota(jnp.int32, (rows, W), 1) < width

    loads[0].wait()
    rows = []
    for t in (leaf + 1, 3, 2):
        total = jnp.zeros((PIECE, W), F32)
        for u in range(SLOTS):
            total = total + jnp.where(tgt_s[u] == t, 1.0, 0.0) * upd_v[u].astype(F32)
        rows.append(total)
    stacked = jnp.where(live(3 * PIECE), jnp.concatenate(rows, axis=0), 0.0).astype(BF16)
    loads[1].wait()
    coupling = jnp.where(live(3 * PIECE), product(stacked, inv_v[...]), 0.0).astype(BF16)
    mats[0, z, y, c] = coupling[:PIECE]

    @pl.when(leaf != 2)
    def _():
        mats[1, z, y, c] = coupling[PIECE : 2 * PIECE]

    part_out[3] = coupling[2 * PIECE :]
    loads[2].wait()
    pl.semaphore_wait(barrier, GRID - 1 + 3)

    def block(j, h, i1, i2):
        if h == 0:
            return mats.at[j, i1 % LINE, i2 % LINE, c, :, pl.ds(0, HALF)]
        return mats.at[j, i2 % LINE, i1 % LINE, c, :, pl.ds(HALF, HALF)]

    def bundle(j, h, i2, core):
        if h == 0:
            return mats.at[j, :, i2 % LINE, core, :, pl.ds(0, HALF)]
        return mats.at[j, i2 % LINE, :, core, :, pl.ds(HALF, HALF)]

    def there(h, i1, i2, core):
        return device(leaf, i1, i2, core) if h == 0 else device(leaf, i2, i1, core)

    started = []

    def gather_copy(ref, j, h, slot, to):
        return pltpu.make_async_remote_copy(
            ref, ref, gat_send.at[j, h, slot], gat_recv.at[j, h, slot], device_id=to, device_id_type=MESH
        )

    def send(ref, j, h, slot, to):
        copy = gather_copy(ref, j, h, slot, to)
        copy.start()
        started.append(copy)

    def arrived(ref, j, h, slot):
        gather_copy(ref, j, h, slot, there(0, z, y, 1 - c)).wait_recv()

    def own(h):
        return place if h == 0 else (place[1], place[0])

    def to_sibling(j, h, slot, i2):
        p1, p2 = own(h)
        send(bundle(j, h, i2, c), j, h, slot, there(h, p1, p2, 1 - c))

    def gather_first(j):
        for i, d in enumerate((1, -1, 2)):
            for h in range(2):
                p1, p2 = own(h)
                send(block(j, h, p1, p2), j, h, i, there(h, p1 + d, p2, c))

    def gather_second(j):
        for i, k in enumerate(NEAR):
            for h in range(2):
                p1, p2 = own(h)
                ref = block(j, h, p1 + k, p2)
                if k:
                    arrived(ref, j, h, i - 1)
                for e, d in enumerate((1, -1)):
                    send(ref, j, h, 3 + 2 * i + e, there(h, p1, p2 + d, c))
        for h in range(2):
            to_sibling(j, h, 15, own(h)[1])

    def gather_third(j):
        for i, k in enumerate(NEAR):
            for h in range(2):
                p1, p2 = own(h)
                for e, d in enumerate((1, -1)):
                    ref = block(j, h, p1 + k, p2 - d)
                    arrived(ref, j, h, 3 + 2 * i + e)
                    if i % 2 == e:
                        send(ref, j, h, 11 + i, there(h, p1, p2 + d, c))
        for h in range(2):
            p2 = own(h)[1]
            to_sibling(j, h, 16, p2 - 1)
            to_sibling(j, h, 17, p2 + 1)

    def gather_last(j):
        for h in range(2):
            p1, p2 = own(h)
            for i, k in enumerate(NEAR):
                arrived(block(j, h, p1 + k, p2 + 2), j, h, 11 + i)
            to_sibling(j, h, 18, p2 + 2)

    def gather_wait(j):
        for h in range(2):
            p2 = own(h)[1]
            for slot, d in ((15, 0), (16, -1), (17, 1), (18, 2)):
                arrived(bundle(j, h, p2 + d, 1 - c), j, h, slot)

    def exchange(source, target, sem):
        def one(d, carry):
            to = (g + d) % GRID
            pltpu.make_async_remote_copy(
                source(to), target.at[g], all_send.at[sem], all_recv.at[sem], device_id=(leaf, to), device_id_type=MESH
            ).start()
            return carry

        lax.fori_loop(1, GRID, one, 0)

    def exchange_wait(target, sem):
        most = target.at[pl.ds(0, GRID - 1)]
        whole = pltpu.make_async_remote_copy(
            most, most, all_send.at[sem], all_recv.at[sem], device_id=(leaf, (g + 1) % GRID), device_id_type=MESH
        )
        whole.wait_recv()
        whole.wait_send()

    def rhs_columns(to):
        return rhs_v.at[:, pl.ds(pl.multiple_of((to // 4) * 128, 128), 128)]

    def hop(source, target, slot, x):
        return pltpu.make_async_remote_copy(
            source, target, hop_send.at[slot], hop_recv.at[slot], device_id=(x, g), device_id_type=MESH
        )

    move = hop(part_out.at[3], mats.at[1, z, y, c], 3, 2)

    gather_first(0)

    @pl.when(leaf == 0)
    def _():
        move.start()

    exchange(rhs_columns, rbuf, 0)
    rbuf[g] = rhs_v[:, pl.ds(pl.multiple_of((g // 4) * 128, 128), 128)]
    gather_second(0)
    gather_third(0)

    @pl.when(leaf == 2)
    def _():
        move.wait_recv()

    gather_first(1)
    exchange_wait(rbuf, 0)
    wide[...] = rbuf[...].reshape(W, 128).astype(F32).T
    mine = pl.ds(pl.multiple_of((g % 4) * PIECE, PIECE), PIECE)
    state[0] = wide[mine, :]
    wide[...] = jnp.zeros_like(wide)

    gather_last(0)
    gather_wait(0)

    def matrix(j):
        return mats[j].reshape(W, W)

    down = hop(part_out.at[0], part_in.at[0], 0, (leaf + 1) % 4)
    far = hop(part_out.at[1], part_in.at[1 + leaf % 2], 1 + leaf % 2, 3)
    early = hop(part_out.at[2], part_in.at[1], 8, 2)

    def solve_step():
        corrected = jnp.where(live(PIECE), state[0], 0.0).astype(BF16)
        part_out[2] = corrected

        @pl.when(leaf < 3)
        def _():
            part_out[0] = product(corrected, matrix(0), True).astype(BF16)
            down.start()

    @pl.when(leaf == 0)
    def _():
        solve_step()
        early.start()

    gather_second(1)

    @pl.when(leaf == 1)
    def _():
        down.wait_recv()
        state[0] = state[0] - part_in[0].astype(F32)
        solve_step()

    gather_third(1)
    gather_last(1)
    gather_wait(1)

    @pl.when(leaf < 2)
    def _():
        part_out[1] = product(part_out[2], matrix(1), True).astype(BF16)
        far.start()

    @pl.when(leaf == 2)
    def _():
        early.wait_recv()
        state[0] = state[0] - product(part_in[1], matrix(1), True)
        down.wait_recv()
        state[0] = state[0] - part_in[0].astype(F32)
        solve_step()

    @pl.when(leaf == 3)
    def _():
        hop(part_out.at[1], part_in.at[1], 1, 3).wait_recv()
        hop(part_out.at[1], part_in.at[2], 2, 3).wait_recv()
        state[0] = state[0] - part_in[1].astype(F32) - part_in[2].astype(F32)
        down.wait_recv()
        state[0] = state[0] - part_in[0].astype(F32)
        solve_step()

    forward = jnp.where(live(PIECE), product(part_out[2], inv_v[...], True), 0.0).astype(BF16)
    state[1] = jnp.where(live(PIECE), product(forward, inv_v[...]), 0.0)

    up = hop(part_out.at[4], part_in.at[3], 4, (leaf + 3) % 4)
    far_one = hop(part_out.at[4], part_in.at[4], 5, 1)
    far_zero = hop(part_out.at[4], part_in.at[4], 6, 0)
    side = hop(part_out.at[5], part_in.at[5], 7, 0)

    @pl.when(leaf == 3)
    def _():
        part_out[4] = state[1].astype(BF16)
        up.start()
        far_one.start()
        far_zero.start()

    def spread(piece, staged, target, sem):
        wide[mine, :] = piece.astype(F32)
        staged[...] = wide[...].T.astype(BF16).reshape(GRID, PIECE, 128)
        exchange(lambda to: staged.at[to], target, sem)
        target[g] = staged[g]

    def collect(target, out):
        for k in range(GRID // 4):
            total = target[4 * k]
            for q in range(1, 4):
                total = total + target[4 * k + q]
            out[:, k * 128 : (k + 1) * 128] = total

    spread(forward, fsend, fbuf, 1)

    for copy in started:
        copy.wait_send()

    @pl.when(leaf == 0)
    def _():
        move.wait_send()
        down.wait_send()
        early.wait_send()
        far.wait_send()

    @pl.when(leaf == 1)
    def _():
        down.wait_send()
        far.wait_send()

    @pl.when(leaf == 2)
    def _():
        down.wait_send()

    exchange_wait(fbuf, 1)
    collect(fbuf, fwd_o)

    @pl.when(leaf == 0)
    def _():
        far_zero.wait_recv()

    @pl.when(leaf == 1)
    def _():
        far_one.wait_recv()

    @pl.when(leaf < 2)
    def _():
        state[1] = state[1] - product(part_in[4], matrix(1))

    @pl.when(leaf == 0)
    def _():
        side.wait_recv()
        state[1] = state[1] - part_in[5].astype(F32)

    @pl.when(leaf < 3)
    def _():
        up.wait_recv()
        part_out[4] = (state[1] - product(part_in[3], matrix(0))).astype(BF16)

    @pl.when((leaf == 1) | (leaf == 2))
    def _():
        up.start()

    @pl.when(leaf == 2)
    def _():
        part_out[5] = product(part_out[4], matrix(1)).astype(BF16)
        side.start()

    spread(part_out[4], osend, obuf, 2)
    exchange_wait(obuf, 2)
    collect(obuf, sol_o)

    @pl.when(leaf > 0)
    def _():
        up.wait_send()

    @pl.when(leaf == 2)
    def _():
        side.wait_send()

    @pl.when(leaf == 3)
    def _():
        far_one.wait_send()
        far_zero.wait_send()


def local(rhs, inverse_blocks, update_blocks, targets, widths):
    hbm = pl.BlockSpec(memory_space=pl.ANY)
    smem = pl.BlockSpec(memory_space=pltpu.SMEM)
    vmem = pl.BlockSpec(memory_space=pltpu.VMEM)
    dma = pltpu.SemaphoreType.DMA
    forward, solved = pl.pallas_call(
        kernel,
        out_shape=(jax.ShapeDtypeStruct((PIECE, W), BF16),) * 2,
        in_specs=[hbm, hbm, hbm, smem, smem],
        out_specs=(vmem, vmem),
        scratch_shapes=[
            pltpu.VMEM((PIECE, W), BF16),
            pltpu.VMEM((W, W), BF16),
            pltpu.VMEM((SLOTS, PIECE, W), BF16),
            pltpu.VMEM((2, LINE, LINE, 2, PIECE, W), BF16),
            pltpu.VMEM((GRID, PIECE, 128), BF16),
            pltpu.VMEM((GRID, PIECE, 128), BF16),
            pltpu.VMEM((GRID, PIECE, 128), BF16),
            pltpu.VMEM((128, W), F32),
            pltpu.VMEM((GRID, PIECE, 128), BF16),
            pltpu.VMEM((GRID, PIECE, 128), BF16),
            pltpu.VMEM((6, PIECE, W), BF16),
            pltpu.VMEM((6, PIECE, W), BF16),
            pltpu.VMEM((2, PIECE, W), F32),
            dma((3,)),
            dma((2, 2, 19)),
            dma((2, 2, 19)),
            dma((3,)),
            dma((3,)),
            dma((9,)),
            dma((9,)),
        ],
        compiler_params=pltpu.CompilerParams(
            collective_id=0, has_side_effects=True, vmem_limit_bytes=48 << 20
        ),
        name="solve",
    )(rhs[0], inverse_blocks[0], update_blocks[0], targets[0, :, 0], widths)
    return forward[None], solved[None]


def solution(mesh):
    placed = (
        P("leaf", "grid", None),
        P("leaf", None, None),
        P("leaf", None, "grid", None),
        P("leaf", None, "grid"),
        P("leaf"),
    )
    return jax.shard_map(
        local,
        mesh=mesh,
        in_specs=placed,
        out_specs=(P("leaf", "grid", None), P("leaf", "grid", None)),
        check_vma=False,
    )
```

time: 788 us -> 66 us (0.08)
  waiting for transfers between devices: 664 us -> 0 us
  Pallas kernels: 0 us -> 59 us
  matrix products: 58.5 us -> 0 us
  local copies, waits for them, and re-layouts: 24.6 us -> 5.38 us
  starting transfers between devices: 14.2 us -> 0 us
  between operations: 15.4 us -> 1.3 us
  other arithmetic: 10.8 us -> 0 us
    psum x4 -> x0, waiting for transfers between devices: 435 us -> none  [local(): coupled = lax.psum(local_term, 'grid')]
    all_gather x4 -> x0, waiting for transfers between devices: 172 us -> none  [local(): lax.all_gather(corrected, 'grid', axis=0, tiled=True)]
    pallas_call x0 -> x1, Pallas kernels: none -> 59 us  [local(): pl.pallas_call(kernel, out_shape=(jax.ShapeDtypeStruct((PIECE, W), BF16),...]
    dot_general x22 -> x0, matrix products: 58.5 us -> none  [the longest x4 22.2 us: local(): lax.dot_general(inverse_rows, weighted, (((0,), (0,)), ((), ())), preferr...]
    ppermute x6 -> x0, waiting for transfers between devices: 56.3 us -> none  [from_behind(): lax.ppermute(value, axis, [(source, source + steps) for source in range(f...]
    ppermute x6 -> x0, starting transfers between devices: 13.5 us -> none  [from_behind(): lax.ppermute(value, axis, [(source, source + steps) for source in range(f...]
    convert_element_type x7 -> x0, local copies, waits for them, and re-layouts: 13 us -> none  [the longest x3 11.9 us: local(): jnp.where(live_full[member], solved_all, 0.0).astype(jnp.bfloat16)]
  transfers between devices with their start and end apart: 14 -> 0, of which waited for: 14 -> 0; matrix products, arithmetic and copies ran while one was open for 4% -> 0% of each run, Pallas kernels for 0% -> 0%
where the time goes in v1:
time: 66 us; the launch traced here: 65.7 us
  Pallas kernels  59 us (89%)
  local copies, waits for them, and re-layouts  5.38 us (8%)
  between operations  1.3 us (2%)
    pallas_call x1, Pallas kernels, local(): pl.pallas_call(kernel, out_shape=(jax.ShapeDtypeStruct((PIECE, W), BF16),...  59 us
    unnamed x10, local copies, waits for them, and re-layouts  5.38 us

profile of v1, /device:TPU:1, one launch (start us, length us, event | category | flops | bytes accessed | tf_op | source)
XLA Modules:
  0.0 65.7 jit_solution(2511262878360851024)
XLA Ops:
  1.3 0.0 copy-start
  1.3 1.6 %copy-done = bf16[1,1024,1024]{2,1,0:T(8,128)(2,1)S(1)} copy-done((bf16[1,1024,1024]{2,1,0:T(8,128)(2,1)S(1)}, bf16[1,1024,1024]{2,1,0:T(8,128)(2,1)}, u32[]{:S(2)}) %copy-start) | copy-done | bytes 2097176
  2.9 0.0 copy-start.1
  2.9 1.0 %copy-done.1 = bf16[1,8,32,1024]{3,2,1,0:T(8,128)(2,1)S(1)} copy-done((bf16[1,8,32,1024]{3,2,1,0:T(8,128)(2,1)S(1)}, bf16[1,8,32,1024]{3,2,1,0:T(8,128)(2,1)}, u32[]{:S(2)}) %copy-start.1) | copy-done | bytes 524312
  3.9 0.0 copy-start.2
  3.9 0.8 %copy-done.2 = bf16[1,32,1024]{2,1,0:T(8,128)(2,1)S(1)} copy-done((bf16[1,32,1024]{2,1,0:T(8,128)(2,1)S(1)}, bf16[1,32,1024]{2,1,0:T(8,128)(2,1)}, u32[]{:S(2)}) %copy-start.2) | copy-done | bytes 65560
  4.8 0.0 copy-start.3
  4.8 0.7 copy-done.3
  5.4 59.0 %solve.1 = (bf16[32,1024]{1,0:T(8,128)(2,1)S(1)}, bf16[32,1024]{1,0:T(8,128)(2,1)S(1)}) custom-call(bf16[32,1024]{1,0:T(8,128)(2,1)S(1)} %bitcast.8, bf16[1024,1024]{1,0:T(8,128)(2,1)S(1)} %bitcast.6, bf16[8,32,1024]{2,1,0:T(8,128)(2,1)S(1)} %bitcast.7, s32[8]{0:T(128)S(1)} %bitcast.11, s32[1]{0:T(128)S(6)} %copy.9.wid_s), custom_call_target="tpu_custom_call" | custom-call | tf_op jit(solution)/shard_map/solve/pallas_call | solution.py:376
  64.5 0.6 copy.10
  65.1 0.6 copy.11
Async XLA Ops:
  1.3 1.6 %copy-start = (bf16[1,1024,1024]{2,1,0:T(8,128)(2,1)S(1)}, bf16[1,1024,1024]{2,1,0:T(8,128)(2,1)}, u32[]{:S(2)}) copy-start(bf16[1,1024,1024]{2,1,0:T(8,128)(2,1)} %param.6) | copy-start | bytes 6291460
  2.9 1.0 %copy-start.1 = (bf16[1,8,32,1024]{3,2,1,0:T(8,128)(2,1)S(1)}, bf16[1,8,32,1024]{3,2,1,0:T(8,128)(2,1)}, u32[]{:S(2)}) copy-start(bf16[1,8,32,1024]{3,2,1,0:T(8,128)(2,1)} %param.7) | copy-start | bytes 1572868
  3.9 0.8 %copy-start.2 = (bf16[1,32,1024]{2,1,0:T(8,128)(2,1)S(1)}, bf16[1,32,1024]{2,1,0:T(8,128)(2,1)}, u32[]{:S(2)}) copy-start(bf16[1,32,1024]{2,1,0:T(8,128)(2,1)} %param.5) | copy-start | bytes 196612
  4.8 0.7 copy-start.3

commit v2 on v1

--- a/solution.py
+++ b/solution.py
@@ -23,9 +23,9 @@
 
 
 def kernel(
-    rhs_h, inv_h, upd_h, tgt_s, wid_s, fwd_o, sol_o,
-    rhs_v, inv_v, upd_v, mats, rbuf, fbuf, obuf, wide, fsend, osend,
-    part_out, part_in, state,
+    rhs_h, inv_h, upd_h, tgt_h, wid_h, fwd_o, sol_o,
+    rhs_v, inv_v, upd_v, tgt_s, wid_s, mats, rbuf, fbuf, obuf, wide, fsend, osend,
+    part_out, part_in, state, acc,
     in_sem, gat_send, gat_recv, all_send, all_recv, hop_send, hop_recv,
 ):
     leaf = lax.axis_index("leaf")
@@ -40,6 +40,8 @@
         pltpu.make_async_copy(upd_h, upd_v, in_sem.at[0]),
         pltpu.make_async_copy(inv_h, inv_v, in_sem.at[1]),
         pltpu.make_async_copy(rhs_h, rhs_v, in_sem.at[2]),
+        pltpu.make_async_copy(tgt_h, tgt_s, in_sem.at[3]),
+        pltpu.make_async_copy(wid_h, wid_s, in_sem.at[4]),
     ]
     for load in loads:
         load.start()
@@ -54,6 +56,8 @@
     for d in (1, 2, 3):
         pl.semaphore_signal(barrier, inc=1, device_id=((leaf + d) % 4, g), device_id_type=MESH)
 
+    loads[3].wait()
+    loads[4].wait()
     width = wid_s[0]
 
     def live(rows):
@@ -69,13 +73,24 @@
     stacked = jnp.where(live(3 * PIECE), jnp.concatenate(rows, axis=0), 0.0).astype(BF16)
     loads[1].wait()
     coupling = jnp.where(live(3 * PIECE), product(stacked, inv_v[...]), 0.0).astype(BF16)
-    mats[0, z, y, c] = coupling[:PIECE]
-
-    @pl.when(leaf != 2)
+
+    @pl.when(leaf < 2)
+    def _():
+        mats[0, z, y, c] = coupling[:PIECE]
+
+    @pl.when(leaf == 0)
     def _():
         mats[1, z, y, c] = coupling[PIECE : 2 * PIECE]
-
-    part_out[3] = coupling[2 * PIECE :]
+        part_out[3] = coupling[2 * PIECE :]
+
+    @pl.when(leaf == 1)
+    def _():
+        part_out[3] = coupling[PIECE : 2 * PIECE]
+
+    @pl.when(leaf == 2)
+    def _():
+        part_out[3] = coupling[:PIECE]
+
     loads[2].wait()
     pl.semaphore_wait(barrier, GRID - 1 + 3)
 
@@ -92,17 +107,13 @@
     def there(h, i1, i2, core):
         return device(leaf, i1, i2, core) if h == 0 else device(leaf, i2, i1, core)
 
-    started = []
-
     def gather_copy(ref, j, h, slot, to):
         return pltpu.make_async_remote_copy(
             ref, ref, gat_send.at[j, h, slot], gat_recv.at[j, h, slot], device_id=to, device_id_type=MESH
         )
 
     def send(ref, j, h, slot, to):
-        copy = gather_copy(ref, j, h, slot, to)
-        copy.start()
-        started.append(copy)
+        gather_copy(ref, j, h, slot, to).start()
 
     def arrived(ref, j, h, slot):
         gather_copy(ref, j, h, slot, there(0, z, y, 1 - c)).wait_recv()
@@ -185,24 +196,47 @@
             source, target, hop_send.at[slot], hop_recv.at[slot], device_id=(x, g), device_id_type=MESH
         )
 
-    move = hop(part_out.at[3], mats.at[1, z, y, c], 3, 2)
-
-    gather_first(0)
-
-    @pl.when(leaf == 0)
-    def _():
-        move.start()
+    own_rows = [mats.at[j, z, y, c] for j in range(2)]
+    move_near = hop(part_out.at[3], own_rows[0], 3, jnp.where(leaf == 0, 2, 3))
+    move_far = hop(part_out.at[3], own_rows[1], 4, 3)
+    two_jobs = (leaf == 0) | (leaf == 3)
+
+    @pl.when(leaf == 1)
+    def _():
+        move_far.start()
+
+    @pl.when((leaf == 0) | (leaf == 2))
+    def _():
+        move_near.start()
+
+    @pl.when(leaf < 2)
+    def _():
+        gather_first(0)
 
     exchange(rhs_columns, rbuf, 0)
     rbuf[g] = rhs_v[:, pl.ds(pl.multiple_of((g // 4) * 128, 128), 128)]
+
+    @pl.when(leaf >= 2)
+    def _():
+        move_near.wait_recv()
+        gather_first(0)
+
     gather_second(0)
+
+    @pl.when(leaf == 3)
+    def _():
+        move_far.wait_recv()
+
+    @pl.when(two_jobs)
+    def _():
+        gather_first(1)
+
     gather_third(0)
 
-    @pl.when(leaf == 2)
-    def _():
-        move.wait_recv()
-
-    gather_first(1)
+    @pl.when(two_jobs)
+    def _():
+        gather_second(1)
+
     exchange_wait(rbuf, 0)
     wide[...] = rbuf[...].reshape(W, 128).astype(F32).T
     mine = pl.ds(pl.multiple_of((g % 4) * PIECE, PIECE), PIECE)
@@ -215,37 +249,56 @@
     def matrix(j):
         return mats[j].reshape(W, W)
 
-    down = hop(part_out.at[0], part_in.at[0], 0, (leaf + 1) % 4)
-    far = hop(part_out.at[1], part_in.at[1 + leaf % 2], 1 + leaf % 2, 3)
-    early = hop(part_out.at[2], part_in.at[1], 8, 2)
-
-    def solve_step():
-        corrected = jnp.where(live(PIECE), state[0], 0.0).astype(BF16)
-        part_out[2] = corrected
-
-        @pl.when(leaf < 3)
-        def _():
-            part_out[0] = product(corrected, matrix(0), True).astype(BF16)
-            down.start()
+    LOW, HIGH = pl.ds(0, HALF), pl.ds(HALF, HALF)
+    halves = (LOW, HIGH)
+
+    def half_rows(j, n):
+        return mats[j, 2 * n : 2 * n + 2].reshape(HALF, W)
+
+    def hops(source, target, slot, x):
+        return [hop(source.at[:, part], target.at[:, part], slot + n, x) for n, part in enumerate(halves)]
+
+    down = hops(part_out.at[0], part_in.at[0], 0, leaf + 1 - 2 * (leaf // 3))
+    pass_on = hops(part_out.at[2], part_in.at[0], 0, 3)
+    early = hop(part_out.at[2], part_in.at[1], 2, 2)
+    far = hop(part_out.at[1], part_in.at[1], 5, 3)
+    skip = hop(part_out.at[2], part_in.at[2], 6, 3)
+
+    def correct(part):
+        columns = lax.broadcasted_iota(jnp.int32, (PIECE, HALF), 1) + part.start
+        part_out[2, :, part] = jnp.where(columns < width, state[0, :, part], 0.0).astype(BF16)
 
     @pl.when(leaf == 0)
     def _():
-        solve_step()
+        for part in halves:
+            correct(part)
+        for n, part in enumerate(halves):
+            part_out[0, :, part] = product(part_out[2], half_rows(0, n), True).astype(BF16)
+            down[n].start()
         early.start()
 
-    gather_second(1)
-
     @pl.when(leaf == 1)
     def _():
-        down.wait_recv()
-        state[0] = state[0] - part_in[0].astype(F32)
-        solve_step()
-
-    gather_third(1)
-    gather_last(1)
-    gather_wait(1)
-
-    @pl.when(leaf < 2)
+        down[0].wait_recv()
+        state[0, :, LOW] = state[0, :, LOW] - part_in[0, :, LOW].astype(F32)
+        correct(LOW)
+        acc[...] = product(part_out[2, :, LOW], mats[0, :, :, :, :, LOW].reshape(W, HALF), True)
+        down[1].wait_recv()
+        state[0, :, HIGH] = state[0, :, HIGH] - part_in[0, :, HIGH].astype(F32)
+        correct(HIGH)
+        for n, part in enumerate(halves):
+            rest = product(part_out[2, :, HIGH], mats[0, 2 * n : 2 * n + 2, :, :, :, HIGH].reshape(HALF, HALF), True)
+            part_out[0, :, part] = (acc[:, part] + rest).astype(BF16)
+            down[n].start()
+        skip.start()
+
+    @pl.when(two_jobs)
+    def _():
+        gather_third(1)
+        gather_last(1)
+        gather_wait(1)
+
+    @pl.when(leaf == 0)
     def _():
         part_out[1] = product(part_out[2], matrix(1), True).astype(BF16)
         far.start()
@@ -253,34 +306,36 @@
     @pl.when(leaf == 2)
     def _():
         early.wait_recv()
-        state[0] = state[0] - product(part_in[1], matrix(1), True)
-        down.wait_recv()
-        state[0] = state[0] - part_in[0].astype(F32)
-        solve_step()
+        state[0] = state[0] - product(part_in[1], matrix(0), True)
+        for n, part in enumerate(halves):
+            down[n].wait_recv()
+            state[0, :, part] = state[0, :, part] - part_in[0, :, part].astype(F32)
+            correct(part)
+            pass_on[n].start()
 
     @pl.when(leaf == 3)
     def _():
-        hop(part_out.at[1], part_in.at[1], 1, 3).wait_recv()
-        hop(part_out.at[1], part_in.at[2], 2, 3).wait_recv()
-        state[0] = state[0] - part_in[1].astype(F32) - part_in[2].astype(F32)
-        down.wait_recv()
-        state[0] = state[0] - part_in[0].astype(F32)
-        solve_step()
+        skip.wait_recv()
+        state[0] = state[0] - product(part_in[2], matrix(1), True)
+        far.wait_recv()
+        state[0] = state[0] - part_in[1].astype(F32)
+        pass_on[0].wait_recv()
+        state[0] = state[0] - product(part_in[0, :, LOW], mats[0, :, :, :, :, LOW].reshape(W, HALF), True)
+        pass_on[1].wait_recv()
+        state[0] = state[0] - product(part_in[0, :, HIGH], mats[0, :, :, :, :, HIGH].reshape(W, HALF), True)
+        for part in halves:
+            correct(part)
 
     forward = jnp.where(live(PIECE), product(part_out[2], inv_v[...], True), 0.0).astype(BF16)
     state[1] = jnp.where(live(PIECE), product(forward, inv_v[...]), 0.0)
 
-    up = hop(part_out.at[4], part_in.at[3], 4, (leaf + 3) % 4)
-    far_one = hop(part_out.at[4], part_in.at[4], 5, 1)
-    far_zero = hop(part_out.at[4], part_in.at[4], 6, 0)
-    side = hop(part_out.at[5], part_in.at[5], 7, 0)
-
-    @pl.when(leaf == 3)
-    def _():
-        part_out[4] = state[1].astype(BF16)
-        up.start()
-        far_one.start()
-        far_zero.start()
+    ahead = hop(state.at[1], acc, 7, 3)
+    jump = hops(part_out.at[6], part_in.at[3], 8, 1)
+    up = hops(part_out.at[4], part_in.at[3], 8, 0)
+    last_to_first = hop(part_out.at[4], part_in.at[4], 10, 0)
+    back = hop(part_out.at[6], part_in.at[4], 11, 2)
+    side_one = hop(part_out.at[5], part_in.at[4], 12, 1)
+    side_zero = hop(part_out.at[5], part_in.at[5], 13, 0)
 
     def spread(piece, staged, target, sem):
         wide[mine, :] = piece.astype(F32)
@@ -295,93 +350,111 @@
                 total = total + target[4 * k + q]
             out[:, k * 128 : (k + 1) * 128] = total
 
+    @pl.when(leaf == 2)
+    def _():
+        ahead.start()
+
+    @pl.when(leaf == 3)
+    def _():
+        part_out[4] = state[1].astype(BF16)
+        last_to_first.start()
+        ahead.wait_recv()
+        for n, part in enumerate(halves):
+            term = product(part_out[4], mats[0, :, :, :, :, part].reshape(W, HALF))
+            part_out[6, :, part] = (acc[:, part] - term).astype(BF16)
+            jump[n].start()
+        back.start()
+        part_out[5] = product(part_out[4], matrix(1)).astype(BF16)
+        side_one.start()
+
     spread(forward, fsend, fbuf, 1)
 
-    for copy in started:
-        copy.wait_send()
-
     @pl.when(leaf == 0)
     def _():
-        move.wait_send()
-        down.wait_send()
-        early.wait_send()
-        far.wait_send()
+        last_to_first.wait_recv()
+        state[1] = state[1] - product(part_in[4], matrix(1))
+
+    @pl.when(leaf < 2)
+    def _():
+        up[0].wait_recv()
+        acc[...] = state[1] - product(part_in[3, :, LOW], half_rows(0, 0))
 
     @pl.when(leaf == 1)
     def _():
-        down.wait_send()
-        far.wait_send()
+        side_one.wait_recv()
+        acc[...] = acc[...] - part_in[4].astype(F32)
+
+    @pl.when(leaf == 0)
+    def _():
+        side_zero.wait_recv()
+        acc[...] = acc[...] - part_in[5].astype(F32)
+
+    @pl.when(leaf < 2)
+    def _():
+        up[1].wait_recv()
+        for n, part in enumerate(halves):
+            term = product(part_in[3, :, HIGH], mats[0, 2:, :, :, :, part].reshape(HALF, HALF))
+            part_out[4, :, part] = (acc[:, part] - term).astype(BF16)
+
+            @pl.when(leaf == 1)
+            def _():
+                up[n].start()
 
     @pl.when(leaf == 2)
     def _():
-        down.wait_send()
+        back.wait_recv()
+        part_out[4] = part_in[4]
+        part_out[5] = product(part_in[4], matrix(0)).astype(BF16)
+        side_zero.start()
+
+    spread(part_out[4], osend, obuf, 2)
 
     exchange_wait(fbuf, 1)
     collect(fbuf, fwd_o)
 
-    @pl.when(leaf == 0)
-    def _():
-        far_zero.wait_recv()
-
-    @pl.when(leaf == 1)
-    def _():
-        far_one.wait_recv()
-
-    @pl.when(leaf < 2)
-    def _():
-        state[1] = state[1] - product(part_in[4], matrix(1))
-
-    @pl.when(leaf == 0)
-    def _():
-        side.wait_recv()
-        state[1] = state[1] - part_in[5].astype(F32)
-
-    @pl.when(leaf < 3)
-    def _():
-        up.wait_recv()
-        part_out[4] = (state[1] - product(part_in[3], matrix(0))).astype(BF16)
-
-    @pl.when((leaf == 1) | (leaf == 2))
-    def _():
-        up.start()
-
-    @pl.when(leaf == 2)
-    def _():
-        part_out[5] = product(part_out[4], matrix(1)).astype(BF16)
-        side.start()
-
-    spread(part_out[4], osend, obuf, 2)
+    def gather_sent(j):
+        for h in range(2):
+            p1, p2 = own(h)
+            for slot in range(19):
+                ref = block(j, h, p1, p2) if slot < 15 else bundle(j, h, p2, c)
+                gather_copy(ref, j, h, slot, there(h, p1, p2, 1 - c)).wait_send()
+
+    gather_sent(0)
+
+    @pl.when(two_jobs)
+    def _():
+        gather_sent(1)
+
+    def sent(when, copies):
+        @pl.when(when)
+        def _():
+            for copy in copies:
+                copy.wait_send()
+
+    sent(leaf == 0, [move_near, *down, early, far])
+    sent(leaf == 1, [move_far, *down, skip, *up])
+    sent(leaf == 2, [move_near, *pass_on, ahead, side_zero])
+    sent(leaf == 3, [last_to_first, *jump, back, side_one])
+
     exchange_wait(obuf, 2)
     collect(obuf, sol_o)
 
-    @pl.when(leaf > 0)
-    def _():
-        up.wait_send()
-
-    @pl.when(leaf == 2)
-    def _():
-        side.wait_send()
-
-    @pl.when(leaf == 3)
-    def _():
-        far_one.wait_send()
-        far_zero.wait_send()
-
 
 def local(rhs, inverse_blocks, update_blocks, targets, widths):
-    hbm = pl.BlockSpec(memory_space=pl.ANY)
-    smem = pl.BlockSpec(memory_space=pltpu.SMEM)
+    hbm = pl.BlockSpec(memory_space=pltpu.HBM)
     vmem = pl.BlockSpec(memory_space=pltpu.VMEM)
     dma = pltpu.SemaphoreType.DMA
     forward, solved = pl.pallas_call(
         kernel,
         out_shape=(jax.ShapeDtypeStruct((PIECE, W), BF16),) * 2,
-        in_specs=[hbm, hbm, hbm, smem, smem],
+        in_specs=[hbm] * 5,
         out_specs=(vmem, vmem),
         scratch_shapes=[
             pltpu.VMEM((PIECE, W), BF16),
             pltpu.VMEM((W, W), BF16),
             pltpu.VMEM((SLOTS, PIECE, W), BF16),
+            pltpu.SMEM((SLOTS,), jnp.int32),
+            pltpu.SMEM((1,), jnp.int32),
             pltpu.VMEM((2, LINE, LINE, 2, PIECE, W), BF16),
             pltpu.VMEM((GRID, PIECE, 128), BF16),
             pltpu.VMEM((GRID, PIECE, 128), BF16),
@@ -389,19 +462,20 @@
             pltpu.VMEM((128, W), F32),
             pltpu.VMEM((GRID, PIECE, 128), BF16),
             pltpu.VMEM((GRID, PIECE, 128), BF16),
-            pltpu.VMEM((6, PIECE, W), BF16),
+            pltpu.VMEM((7, PIECE, W), BF16),
             pltpu.VMEM((6, PIECE, W), BF16),
             pltpu.VMEM((2, PIECE, W), F32),
-            dma((3,)),
+            pltpu.VMEM((PIECE, W), F32),
+            dma((5,)),
             dma((2, 2, 19)),
             dma((2, 2, 19)),
             dma((3,)),
             dma((3,)),
-            dma((9,)),
-            dma((9,)),
+            dma((14,)),
+            dma((14,)),
         ],
         compiler_params=pltpu.CompilerParams(
-            collective_id=0, has_side_effects=True, vmem_limit_bytes=48 << 20
+            collective_id=0, has_side_effects=True, vmem_limit_bytes=60 << 20
         ),
         name="solve",
     )(rhs[0], inverse_blocks[0], update_blocks[0], targets[0, :, 0], widths)

time: 66 us -> 58.3 us (0.88)
  Pallas kernels: 59 us -> 53.8 us
  local copies, waits for them, and re-layouts: 5.38 us -> 2.95 us
    pallas_call x1, Pallas kernels: 59 us -> 53.8 us  [local(): pl.pallas_call(kernel, out_shape=(jax.ShapeDtypeStruct((PIECE, W), BF16),...]
    unnamed x10 -> x2, local copies, waits for them, and re-layouts: 5.38 us -> 2.95 us
where the time goes in v2:
time: 58.3 us; the launch traced here: 58 us
  Pallas kernels  53.8 us (92%)
  local copies, waits for them, and re-layouts  2.95 us (5%)
  between operations  1.29 us (2%)
    pallas_call x1, Pallas kernels, local(): pl.pallas_call(kernel, out_shape=(jax.ShapeDtypeStruct((PIECE, W), BF16),...  53.8 us
    unnamed x2, local copies, waits for them, and re-layouts  2.95 us

profile of v2, /device:TPU:1, one launch (start us, length us, event | category | flops | bytes accessed | tf_op | source)
XLA Modules:
  0.0 58.0 jit_solution(16005268943016060768)
XLA Ops:
  1.3 53.8 %solve.1 = (bf16[32,1024]{1,0:T(8,128)(2,1)}, bf16[32,1024]{1,0:T(8,128)(2,1)}) custom-call(bf16[32,1024]{1,0:T(8,128)(2,1)} %bitcast.8, bf16[1024,1024]{1,0:T(8,128)(2,1)} %bitcast.6, bf16[8,32,1024]{2,1,0:T(8,128)(2,1)} %bitcast.7, s32[8]{0:T(128)} %bitcast.11, s32[1]{0:T(128)S(6)} %copy.9.wid_h), custom_call_target="tpu_custom_call" | custom-call | tf_op jit(solution)/shard_map/solve/pallas_call | solution.py:447
  55.1 1.5 %copy.10 = bf16[1,32,1024]{2,1,0:T(8,128)(2,1)} copy(bf16[1,32,1024]{2,1,0:T(8,128)(2,1)} %bitcast.10) | data formatting | bytes 131072
  56.6 1.5 %copy.11 = bf16[1,32,1024]{2,1,0:T(8,128)(2,1)} copy(bf16[1,32,1024]{2,1,0:T(8,128)(2,1)} %bitcast.9) | data formatting | bytes 131072

commit v3 on v2

v3 whole, which is shorter than its diff:
```python
import jax
import jax.numpy as jnp
from jax import lax
from jax.experimental import pallas as pl
from jax.experimental.pallas import tpu as pltpu
from jax.sharding import PartitionSpec as P

MESH = pl.DeviceIdType.MESH
W = 1024
PIECE = 32
GRID = 32
LINE = 4
SLOTS = 8
HALF = W // 2
NEAR = (0, -1, 1, 2)
F32 = jnp.float32
BF16 = jnp.bfloat16


def product(a, b, transposed=False):
    dims = (((1,), (1 if transposed else 0,)), ((), ()))
    return lax.dot_general(a, b, dims, preferred_element_type=F32)


def kernel(
    rhs_h, inv_h, upd_h, tgt_h, wid_h, fwd_o, sol_o,
    rhs_v, inv_v, upd_v, tgt_s, wid_s, gram, mats, rbuf, fbuf, obuf,
    part_out, part_in, state, acc,
    in_sem, gat_send, gat_recv, all_send, all_recv, hop_send, hop_recv,
):
    leaf = lax.axis_index("leaf")
    g = lax.axis_index("grid")
    z, y, c = g // 8, (g // 2) % LINE, g % 2
    place = (z, y)

    def device(x, zz, yy, cc):
        return (x, ((zz % LINE) * LINE + (yy % LINE)) * 2 + cc)

    loads = [
        pltpu.make_async_copy(upd_h, upd_v, in_sem.at[0]),
        pltpu.make_async_copy(inv_h, inv_v, in_sem.at[1]),
        pltpu.make_async_copy(rhs_h, rhs_v, in_sem.at[2]),
        pltpu.make_async_copy(tgt_h, tgt_s, in_sem.at[3]),
        pltpu.make_async_copy(wid_h, wid_s, in_sem.at[4]),
    ]
    for load in loads:
        load.start()

    barrier = pltpu.get_barrier_semaphore()

    def greet(d, carry):
        pl.semaphore_signal(barrier, inc=1, device_id=(leaf, (g + d) % GRID), device_id_type=MESH)
        return carry

    lax.fori_loop(1, GRID, greet, 0)
    for d in (1, 2, 3):
        pl.semaphore_signal(barrier, inc=1, device_id=((leaf + d) % 4, g), device_id_type=MESH)

    loads[3].wait()
    loads[4].wait()
    width = wid_s[0]

    def live(rows):
        return lax.broadcasted_iota(jnp.int32, (rows, W), 1) < width

    loads[0].wait()

    def rows_for(t):
        total = jnp.zeros((PIECE, W), F32)
        for u in range(SLOTS):
            total = total + jnp.where(tgt_s[u] == t, 1.0, 0.0) * upd_v[u].astype(F32)
        return jnp.where(live(PIECE), total, 0.0).astype(BF16)

    def coupling(stacked):
        size = stacked.shape[0]
        return jnp.where(live(size), product(stacked, inv_v[...]), 0.0).astype(BF16)

    first = rows_for(leaf + 1)
    loads[1].wait()
    mats[jnp.where(leaf < 2, 0, 2), z, y, c] = coupling(first)
    pl.semaphore_wait(barrier, GRID - 1 + 3)

    def block(j, h, i1, i2, core=c):
        if h == 0:
            return mats.at[j, i1 % LINE, i2 % LINE, core, :, pl.ds(0, HALF)]
        return mats.at[j, i2 % LINE, i1 % LINE, core, :, pl.ds(HALF, HALF)]

    def bundle(j, h, i2, core):
        if h == 0:
            return mats.at[j, :, i2 % LINE, core, :, pl.ds(0, HALF)]
        return mats.at[j, i2 % LINE, :, core, :, pl.ds(HALF, HALF)]

    def there(h, i1, i2, core):
        return device(leaf, i1, i2, core) if h == 0 else device(leaf, i2, i1, core)

    def gather_copy(ref, j, h, slot, group, to):
        return pltpu.make_async_remote_copy(
            ref, ref, gat_send.at[j, h, group], gat_recv.at[j, h, slot], device_id=to, device_id_type=MESH
        )

    def send(ref, j, h, slot, group, to):
        gather_copy(ref, j, h, slot, group, to).start()

    def arrived(ref, j, h, slot):
        gather_copy(ref, j, h, slot, 0, there(0, z, y, 1 - c)).wait_recv()

    def own(h):
        return place if h == 0 else (place[1], place[0])

    def sibling(h):
        p1, p2 = own(h)
        return there(h, p1, p2, 1 - c)

    def gather_first(j):
        for i, d in ((2, 2), (0, 1), (1, -1)):
            for h in range(2):
                p1, p2 = own(h)
                send(block(j, h, p1, p2), j, h, i, 0, there(h, p1 + d, p2, c))

    def gather_second(j):
        for i, k in enumerate(NEAR):
            for h in range(2):
                p1, p2 = own(h)
                ref = block(j, h, p1 + k, p2)
                if k:
                    arrived(ref, j, h, i - 1)
                for e, d in enumerate((1, -1)):
                    send(ref, j, h, 3 + 2 * i + e, 1, there(h, p1, p2 + d, c))
        for h in range(2):
            send(bundle(j, h, own(h)[1], c), j, h, 15, 3, sibling(h))

    def gather_third(j):
        for i, k in enumerate(NEAR):
            for h in range(2):
                p1, p2 = own(h)
                for e, d in enumerate((1, -1)):
                    ref = block(j, h, p1 + k, p2 - d)
                    arrived(ref, j, h, 3 + 2 * i + e)
                    if i % 2 == e:
                        send(ref, j, h, 11 + i, 2, there(h, p1, p2 + d, c))
                    send(ref, j, h, 16 + 2 * i + e, 4, sibling(h))

    def gather_last(j):
        for i, k in enumerate(NEAR):
            for h in range(2):
                p1, p2 = own(h)
                ref = block(j, h, p1 + k, p2 + 2)
                arrived(ref, j, h, 11 + i)
                send(ref, j, h, 24 + i, 5, sibling(h))

    def gather_wait(j):
        for h in range(2):
            p1, p2 = own(h)
            arrived(bundle(j, h, p2, 1 - c), j, h, 15)
            for i, k in enumerate(NEAR):
                for e, d in enumerate((1, -1)):
                    arrived(block(j, h, p1 + k, p2 - d, 1 - c), j, h, 16 + 2 * i + e)
        for h in range(2):
            p1, p2 = own(h)
            for i, k in enumerate(NEAR):
                arrived(block(j, h, p1 + k, p2 + 2, 1 - c), j, h, 24 + i)

    def gather_sent(j):
        for h, part in enumerate((pl.ds(0, HALF), pl.ds(HALF, HALF))):
            for group, size in enumerate((3, 8, 4, 4, 8, 4)):
                if size == 8:
                    ref = mats.at[j, pl.ds(0, 2), :, c, :, part]
                else:
                    ref = mats.at[j, 0, pl.ds(0, size), c, :, part]
                gather_copy(ref, j, h, 0, group, sibling(h)).wait_send()

    def exchange(source, target, sem):
        for dz in (2, 1, 3, 0):
            for dy in (2, 1, 3, 0):
                for dc in (1, 0):
                    if dz or dy or dc:
                        to = (((z + dz) % LINE) * LINE + (y + dy) % LINE) * 2 + (c + dc) % 2
                        pltpu.make_async_remote_copy(
                            source(to),
                            target.at[g],
                            all_send.at[sem],
                            all_recv.at[sem],
                            device_id=(leaf, to),
                            device_id_type=MESH,
                        ).start()

    def exchange_wait(target, sem):
        most = target.at[pl.ds(0, GRID - 1)]
        whole = pltpu.make_async_remote_copy(
            most, most, all_send.at[sem], all_recv.at[sem], device_id=(leaf, (g + 1) % GRID), device_id_type=MESH
        )
        whole.wait_recv()
        whole.wait_send()

    def around(device_index):
        return pl.ds(pl.multiple_of((device_index // 4) * 128, 128), 128)

    def spread(source, target, sem):
        exchange(lambda to: source.at[:, around(to)], target, sem)
        target[g] = source[:, around(g)]

    def collect(target):
        lane = lax.broadcasted_iota(jnp.int32, (PIECE, 128), 1)
        row = lax.broadcasted_iota(jnp.int32, (PIECE, 128), 0)
        pick = jnp.where(lane == row + (g % 4) * PIECE, 1.0, 0.0).astype(BF16)
        return product(pick, target[...].reshape(W, 128), True)

    def hop(source, target, slot, x):
        return pltpu.make_async_remote_copy(
            source, target, hop_send.at[slot], hop_recv.at[slot], device_id=(x, g), device_id_type=MESH
        )

    own_rows = [mats.at[j, z, y, c] for j in range(3)]
    move_near = hop(own_rows[2], own_rows[0], 3, jnp.where(leaf == 0, 2, 3))
    move_far = hop(own_rows[2], own_rows[1], 4, 3)
    two_jobs = (leaf == 0) | (leaf == 3)

    @pl.when(leaf < 2)
    def _():
        gather_first(0)

    @pl.when(leaf == 2)
    def _():
        move_near.start()

    @pl.when(leaf < 2)
    def _():
        others = coupling(jnp.concatenate([rows_for(3), rows_for(2)], axis=0))
        near, far = others[:PIECE], others[PIECE:]
        mats[1, z, y, c] = near
        mats[2, z, y, c] = jnp.where(leaf == 0, far, near)

    @pl.when(leaf == 0)
    def _():
        move_near.start()

    @pl.when(leaf == 1)
    def _():
        move_far.start()

    loads[2].wait()
    spread(rhs_v, rbuf, 0)

    @pl.when(leaf >= 2)
    def _():
        def strip(r, carry):
            part = pl.ds(pl.multiple_of(r * 256, 256), 256)
            kept = lax.broadcasted_iota(jnp.int32, (256, W), 0) + r * 256 < width
            inv_v[part, :] = jnp.where(kept, inv_v[part, :].astype(F32), 0.0).astype(BF16)
            return carry

        lax.fori_loop(0, 4, strip, 0)

        def column(r, carry):
            part = pl.ds(pl.multiple_of(r * 256, 256), 256)
            gram[:, part] = lax.dot_general(
                inv_v[...], inv_v[:, part], (((0,), (0,)), ((), ())), preferred_element_type=F32
            ).astype(BF16)
            return carry

        lax.fori_loop(0, 4, column, 0)
        move_near.wait_recv()
        gather_first(0)

    gather_second(0)

    @pl.when(leaf == 3)
    def _():
        move_far.wait_recv()

    @pl.when(two_jobs)
    def _():
        gather_first(1)

    gather_third(0)

    @pl.when(two_jobs)
    def _():
        gather_second(1)

    exchange_wait(rbuf, 0)
    state[0] = collect(rbuf)

    gather_last(0)
    gather_wait(0)

    def matrix(j):
        return mats[j].reshape(W, W)

    LOW, HIGH = pl.ds(0, HALF), pl.ds(HALF, HALF)
    halves = (LOW, HIGH)

    def half_rows(j, n):
        return mats[j, 2 * n : 2 * n + 2].reshape(HALF, W)

    def hops(source, target, slot, x):
        return [hop(source.at[:, part], target.at[:, part], slot + n, x) for n, part in enumerate(halves)]

    down = hops(part_out.at[0], part_in.at[0], 0, leaf + 1 - 2 * (leaf // 3))
    pass_on = hops(part_out.at[2], part_in.at[0], 0, 3)
    early = hop(part_out.at[2], part_in.at[1], 2, 2)
    far = hop(part_out.at[1], part_in.at[1], 5, 3)
    skip = hop(part_out.at[2], part_in.at[2], 6, 3)

    def correct(part):
        columns = lax.broadcasted_iota(jnp.int32, (PIECE, HALF), 1) + part.start
        part_out[2, :, part] = jnp.where(columns < width, state[0, :, part], 0.0).astype(BF16)

    @pl.when(leaf == 0)
    def _():
        for part in halves:
            correct(part)
        for n, part in enumerate(halves):
            part_out[0, :, part] = product(part_out[2], half_rows(0, n), True).astype(BF16)
            down[n].start()
        early.start()

    @pl.when(leaf < 2)
    def _():
        gather_first(2)

    @pl.when(leaf == 1)
    def _():
        down[0].wait_recv()
        state[0, :, LOW] = state[0, :, LOW] - part_in[0, :, LOW].astype(F32)
        correct(LOW)
        acc[...] = product(part_out[2, :, LOW], mats[0, :, :, :, :, LOW].reshape(W, HALF), True)
        down[1].wait_recv()
        state[0, :, HIGH] = state[0, :, HIGH] - part_in[0, :, HIGH].astype(F32)
        correct(HIGH)
        for n, part in enumerate(halves):
            rest = product(part_out[2, :, HIGH], mats[0, 2 * n : 2 * n + 2, :, :, :, HIGH].reshape(HALF, HALF), True)
            part_out[0, :, part] = (acc[:, part] + rest).astype(BF16)
            down[n].start()
        skip.start()

    @pl.when(two_jobs)
    def _():
        gather_third(1)

    @pl.when(leaf < 2)
    def _():
        gather_second(2)

    @pl.when(two_jobs)
    def _():
        gather_last(1)
        gather_wait(1)

    @pl.when(leaf == 0)
    def _():
        part_out[1] = product(part_out[2], matrix(1), True).astype(BF16)
        far.start()

    @pl.when(leaf == 2)
    def _():
        early.wait_recv()
        state[0] = state[0] - product(part_in[1], matrix(0), True)
        for n, part in enumerate(halves):
            down[n].wait_recv()
            state[0, :, part] = state[0, :, part] - part_in[0, :, part].astype(F32)
            correct(part)
            pass_on[n].start()

    @pl.when(leaf == 3)
    def _():
        skip.wait_recv()
        state[0] = state[0] - product(part_in[2], matrix(1), True)
        far.wait_recv()
        state[0] = state[0] - part_in[1].astype(F32)
        pass_on[0].wait_recv()
        state[0] = state[0] - product(part_in[0, :, LOW], mats[0, :, :, :, :, LOW].reshape(W, HALF), True)
        pass_on[1].wait_recv()
        state[0] = state[0] - product(part_in[0, :, HIGH], mats[0, :, :, :, :, HIGH].reshape(W, HALF), True)
        for part in halves:
            correct(part)

    ahead = hops(part_out.at[5], part_in.at[5], 14, 3)
    jump = hops(part_out.at[6], part_in.at[3], 8, 1)
    up = hops(part_out.at[4], part_in.at[3], 8, 0)
    last_to_zero = hop(part_out.at[4], part_in.at[4], 10, 0)
    last_to_one = hop(part_out.at[4], part_in.at[4], 12, 1)
    back = hop(part_out.at[6], part_in.at[4], 11, 2)
    across = hop(part_out.at[6], part_in.at[5], 13, 0)

    @pl.when(leaf == 2)
    def _():
        for n, part in enumerate(halves):
            columns = lax.broadcasted_iota(jnp.int32, (PIECE, HALF), 1) + part.start
            own_part = jnp.where(columns < width, product(part_out[2], gram[:, part]), 0.0)
            part_out[5, :, part] = own_part.astype(BF16)
            ahead[n].start()

    @pl.when(leaf == 3)
    def _():
        part_out[4] = jnp.where(live(PIECE), product(part_out[2], gram[...]), 0.0).astype(BF16)
        last_to_one.start()
        for n, part in enumerate(halves):
            term = product(part_out[4], mats[0, :, :, :, :, part].reshape(W, HALF))
            ahead[n].wait_recv()
            part_out[6, :, part] = (part_in[5, :, part].astype(F32) - term).astype(BF16)
            jump[n].start()
        last_to_zero.start()
        across.start()
        back.start()

    forward = jnp.where(live(PIECE), product(part_out[2], inv_v[...], True), 0.0).astype(BF16)

    @pl.when(leaf < 2)
    def _():
        state[1] = jnp.where(live(PIECE), product(forward, inv_v[...]), 0.0)
        gather_third(2)

    part_out[7] = forward
    spread(part_out.at[7], fbuf, 1)

    @pl.when(leaf < 2)
    def _():
        gather_last(2)
        gather_wait(2)

    @pl.when(leaf == 0)
    def _():
        last_to_zero.wait_recv()
        state[1] = state[1] - product(part_in[4], matrix(1))
        across.wait_recv()
        state[1] = state[1] - product(part_in[5], matrix(2))

    @pl.when(leaf == 1)
    def _():
        last_to_one.wait_recv()
        state[1] = state[1] - product(part_in[4], matrix(2))

    @pl.when(leaf < 2)
    def _():
        up[0].wait_recv()
        acc[...] = state[1] - product(part_in[3, :, LOW], half_rows(0, 0))
        up[1].wait_recv()
        for n, part in enumerate(halves):
            term = product(part_in[3, :, HIGH], mats[0, 2:, :, :, :, part].reshape(HALF, HALF))
            part_out[4, :, part] = (acc[:, part] - term).astype(BF16)

            @pl.when(leaf == 1)
            def _():
                up[n].start()

    @pl.when(leaf == 2)
    def _():
        back.wait_recv()
        part_out[4] = part_in[4]

    spread(part_out.at[4], obuf, 2)

    exchange_wait(fbuf, 1)
    fwd_o[...] = collect(fbuf).astype(BF16)

    gather_sent(0)

    @pl.when(two_jobs)
    def _():
        gather_sent(1)

    @pl.when(leaf < 2)
    def _():
        gather_sent(2)

    def sent(when, copies):
        @pl.when(when)
        def _():
            for copy in copies:
                copy.wait_send()

    sent(leaf == 0, [move_near, *down, early, far])
    sent(leaf == 1, [move_far, *down, skip, *up])
    sent(leaf == 2, [move_near, *pass_on, *ahead])
    sent(leaf == 3, [last_to_one, *jump, last_to_zero, across, back])

    exchange_wait(obuf, 2)
    sol_o[...] = collect(obuf).astype(BF16)


def local(rhs, inverse_blocks, update_blocks, targets, widths):
    hbm = pl.BlockSpec(memory_space=pltpu.HBM)
    vmem = pl.BlockSpec(memory_space=pltpu.VMEM)
    dma = pltpu.SemaphoreType.DMA
    forward, solved = pl.pallas_call(
        kernel,
        out_shape=(jax.ShapeDtypeStruct((PIECE, W), BF16),) * 2,
        in_specs=[hbm] * 5,
        out_specs=(vmem, vmem),
        scratch_shapes=[
            pltpu.VMEM((PIECE, W), BF16),
            pltpu.VMEM((W, W), BF16),
            pltpu.VMEM((SLOTS, PIECE, W), BF16),
            pltpu.SMEM((SLOTS,), jnp.int32),
            pltpu.SMEM((1,), jnp.int32),
            pltpu.VMEM((W, W), BF16),
            pltpu.VMEM((3, LINE, LINE, 2, PIECE, W), BF16),
            pltpu.VMEM((GRID, PIECE, 128), BF16),
            pltpu.VMEM((GRID, PIECE, 128), BF16),
            pltpu.VMEM((GRID, PIECE, 128), BF16),
            pltpu.VMEM((8, PIECE, W), BF16),
            pltpu.VMEM((6, PIECE, W), BF16),
            pltpu.VMEM((2, PIECE, W), F32),
            pltpu.VMEM((PIECE, W), F32),
            dma((5,)),
            dma((3, 2, 6)),
            dma((3, 2, 28)),
            dma((3,)),
            dma((3,)),
            dma((16,)),
            dma((16,)),
        ],
        compiler_params=pltpu.CompilerParams(
            collective_id=0, has_side_effects=True, vmem_limit_bytes=55040 << 10
        ),
        name="solve",
    )(rhs[0], inverse_blocks[0], update_blocks[0], targets[0, :, 0], widths)
    return forward[None], solved[None]


def solution(mesh):
    placed = (
        P("leaf", "grid", None),
        P("leaf", None, None),
        P("leaf", None, "grid", None),
        P("leaf", None, "grid"),
        P("leaf"),
    )
    return jax.shard_map(
        local,
        mesh=mesh,
        in_specs=placed,
        out_specs=(P("leaf", "grid", None), P("leaf", "grid", None)),
        check_vma=False,
    )
```

time: 58.3 us -> 55.6 us (0.954)
  Pallas kernels: 53.8 us -> 52.2 us
  local copies, waits for them, and re-layouts: 2.95 us -> 1.91 us
    pallas_call x1, Pallas kernels: 53.8 us -> 52.2 us  [local(): pl.pallas_call(kernel, out_shape=(jax.ShapeDtypeStruct((PIECE, W), BF16),...]
    unnamed x2 -> x4, local copies, waits for them, and re-layouts: 2.95 us -> 1.91 us
where the time goes in v3:
time: 55.6 us; the launch traced here: 55.4 us
  Pallas kernels  52.2 us (94%)
  local copies, waits for them, and re-layouts  1.91 us (3%)
  between operations  1.29 us (2%)
    pallas_call x1, Pallas kernels, local(): pl.pallas_call(kernel, out_shape=(jax.ShapeDtypeStruct((PIECE, W), BF16),...  52.2 us
    unnamed x4, local copies, waits for them, and re-layouts  1.91 us

profile of v3, /device:TPU:1, one launch (start us, length us, event | category | flops | bytes accessed | tf_op | source)
XLA Modules:
  0.0 55.4 jit_solution(7224528254743637028)
XLA Ops:
  1.3 0.0 copy-start
  1.3 0.6 %copy-done = s32[1,8,1]{1,2,0:T(1,128)S(1)} copy-done((s32[1,8,1]{1,2,0:T(1,128)S(1)}, s32[1,8,1]{1,2,0:T(1,128)}, u32[]{:S(2)}) %copy-start) | copy-done | bytes 56
  1.9 52.2 %solve.1 = (bf16[32,1024]{1,0:T(8,128)(2,1)S(1)}, bf16[32,1024]{1,0:T(8,128)(2,1)S(1)}) custom-call(bf16[32,1024]{1,0:T(8,128)(2,1)} %bitcast.11, bf16[1024,1024]{1,0:T(8,128)(2,1)} %bitcast.9, bf16[8,32,1024]{2,1,0:T(8,128)(2,1)} %bitcast.10, s32[8]{0:T(128)S(1)} %bitcast.8, s32[1]{0:T(128)S(6)} %copy.9.wid_h), custom_call_target="tpu_custom_call" | custom-call | tf_op jit(solution)/shard_map/solve/pallas_call | solution.py:486
  54.2 0.6 %copy.10 = bf16[1,32,1024]{2,1,0:T(8,128)(2,1)} copy(bf16[1,32,1024]{2,1,0:T(8,128)(2,1)S(1)} %bitcast.7) | data formatting | bytes 131072
  54.8 0.6 %copy.11 = bf16[1,32,1024]{2,1,0:T(8,128)(2,1)} copy(bf16[1,32,1024]{2,1,0:T(8,128)(2,1)S(1)} %bitcast.6) | data formatting | bytes 131072
Async XLA Ops:
  1.3 0.7 %copy-start = (s32[1,8,1]{1,2,0:T(1,128)S(1)}, s32[1,8,1]{1,2,0:T(1,128)}, u32[]{:S(2)}) copy-start(s32[1,8,1]{1,2,0:T(1,128)} %param.8) | copy-start | bytes 100

commit v4 on v3

--- a/solution.py
+++ b/solution.py
@@ -13,6 +13,7 @@
 SLOTS = 8
 HALF = W // 2
 NEAR = (0, -1, 1, 2)
+OTHERS = [(dz, dy, dc) for dz in (2, 1, 3, 0) for dy in (2, 1, 3, 0) for dc in (1, 0) if dz or dy or dc]
 F32 = jnp.float32
 BF16 = jnp.bfloat16
 
@@ -24,7 +25,7 @@
 
 def kernel(
     rhs_h, inv_h, upd_h, tgt_h, wid_h, fwd_o, sol_o,
-    rhs_v, inv_v, upd_v, tgt_s, wid_s, gram, mats, rbuf, fbuf, obuf,
+    rhs_v, inv_v, upd_v, tgt_s, wid_s, gram, mats, rbuf, fbuf, obuf, packs,
     part_out, part_in, state, acc,
     in_sem, gat_send, gat_recv, all_send, all_recv, hop_send, hop_recv,
 ):
@@ -48,13 +49,11 @@
 
     barrier = pltpu.get_barrier_semaphore()
 
-    def greet(d, carry):
-        pl.semaphore_signal(barrier, inc=1, device_id=(leaf, (g + d) % GRID), device_id_type=MESH)
-        return carry
-
-    lax.fori_loop(1, GRID, greet, 0)
-    for d in (1, 2, 3):
+    for d in (2, 1, 3):
         pl.semaphore_signal(barrier, inc=1, device_id=((leaf + d) % 4, g), device_id_type=MESH)
+    for dz, dy, dc in OTHERS:
+        to = device(leaf, z + dz, y + dy, (c + dc) % 2)
+        pl.semaphore_signal(barrier, inc=1, device_id=to, device_id_type=MESH)
 
     loads[3].wait()
     loads[4].wait()
@@ -170,19 +169,16 @@
                 gather_copy(ref, j, h, 0, group, sibling(h)).wait_send()
 
     def exchange(source, target, sem):
-        for dz in (2, 1, 3, 0):
-            for dy in (2, 1, 3, 0):
-                for dc in (1, 0):
-                    if dz or dy or dc:
-                        to = (((z + dz) % LINE) * LINE + (y + dy) % LINE) * 2 + (c + dc) % 2
-                        pltpu.make_async_remote_copy(
-                            source(to),
-                            target.at[g],
-                            all_send.at[sem],
-                            all_recv.at[sem],
-                            device_id=(leaf, to),
-                            device_id_type=MESH,
-                        ).start()
+        for dz, dy, dc in OTHERS:
+            to = device(leaf, z + dz, y + dy, (c + dc) % 2)
+            pltpu.make_async_remote_copy(
+                source(to[1]),
+                target.at[g],
+                all_send.at[sem],
+                all_recv.at[sem],
+                device_id=to,
+                device_id_type=MESH,
+            ).start()
 
     def exchange_wait(target, sem):
         most = target.at[pl.ds(0, GRID - 1)]
@@ -195,15 +191,25 @@
     def around(device_index):
         return pl.ds(pl.multiple_of((device_index // 4) * 128, 128), 128)
 
-    def spread(source, target, sem):
-        exchange(lambda to: source.at[:, around(to)], target, sem)
-        target[g] = source[:, around(g)]
+    def spread(values, packed, target, sem):
+        left = lax.broadcasted_iota(jnp.int32, (16, 128), 1) < 64
+        for k in range(GRID // 4):
+            tile = values[:, k * 128 : (k + 1) * 128].astype(F32)
+            top, bottom = tile[:16], tile[16:]
+            part = pl.ds(k * 128, 128)
+            packed[0, :, part] = jnp.where(left, top, pltpu.roll(bottom, 64, 1)).astype(BF16)
+            packed[1, :, part] = jnp.where(left, pltpu.roll(top, 64, 1), bottom).astype(BF16)
+        exchange(lambda to: packed.at[(to % 4) // 2, :, around(to)], target, sem)
+        target[g] = packed[(g % 4) // 2, :, around(g)]
 
     def collect(target):
         lane = lax.broadcasted_iota(jnp.int32, (PIECE, 128), 1)
         row = lax.broadcasted_iota(jnp.int32, (PIECE, 128), 0)
-        pick = jnp.where(lane == row + (g % 4) * PIECE, 1.0, 0.0).astype(BF16)
-        return product(pick, target[...].reshape(W, 128), True)
+        pick = jnp.where(lane == row + (g % 2) * PIECE, 1.0, 0.0).astype(BF16)
+        held = target[...].astype(F32)
+        turned = pltpu.roll(held.reshape(GRID * 16, 128), 64, 1).reshape(GRID, 16, 128)
+        whole = jnp.concatenate([held, turned], axis=1).reshape(W, 128).astype(BF16)
+        return product(pick, whole, True)
 
     def hop(source, target, slot, x):
         return pltpu.make_async_remote_copy(
@@ -239,7 +245,7 @@
         move_far.start()
 
     loads[2].wait()
-    spread(rhs_v, rbuf, 0)
+    spread(rhs_v[...], packs.at[0], rbuf, 0)
 
     @pl.when(leaf >= 2)
     def _():
@@ -411,8 +417,7 @@
         state[1] = jnp.where(live(PIECE), product(forward, inv_v[...]), 0.0)
         gather_third(2)
 
-    part_out[7] = forward
-    spread(part_out.at[7], fbuf, 1)
+    spread(forward, packs.at[1], fbuf, 1)
 
     @pl.when(leaf < 2)
     def _():
@@ -449,7 +454,7 @@
         back.wait_recv()
         part_out[4] = part_in[4]
 
-    spread(part_out.at[4], obuf, 2)
+    spread(part_out[4], packs.at[2], obuf, 2)
 
     exchange_wait(fbuf, 1)
     fwd_o[...] = collect(fbuf).astype(BF16)
@@ -496,10 +501,11 @@
             pltpu.SMEM((1,), jnp.int32),
             pltpu.VMEM((W, W), BF16),
             pltpu.VMEM((3, LINE, LINE, 2, PIECE, W), BF16),
-            pltpu.VMEM((GRID, PIECE, 128), BF16),
-            pltpu.VMEM((GRID, PIECE, 128), BF16),
-            pltpu.VMEM((GRID, PIECE, 128), BF16),
-            pltpu.VMEM((8, PIECE, W), BF16),
+            pltpu.VMEM((GRID, 16, 128), BF16),
+            pltpu.VMEM((GRID, 16, 128), BF16),
+            pltpu.VMEM((GRID, 16, 128), BF16),
+            pltpu.VMEM((3, 2, 16, W), BF16),
+            pltpu.VMEM((7, PIECE, W), BF16),
             pltpu.VMEM((6, PIECE, W), BF16),
             pltpu.VMEM((2, PIECE, W), F32),
             pltpu.VMEM((PIECE, W), F32),

time: 55.6 us -> 54.1 us (0.973)
  Pallas kernels: 52.2 us -> 50.8 us
    pallas_call x1, Pallas kernels: 52.2 us -> 50.8 us  [local(): pl.pallas_call(kernel, out_shape=(jax.ShapeDtypeStruct((PIECE, W), BF16),...]
where the time goes in v4:
time: 54.1 us; the launch traced here: 54 us
  Pallas kernels  50.8 us (94%)
  local copies, waits for them, and re-layouts  1.91 us (4%)
  between operations  1.29 us (2%)
    pallas_call x1, Pallas kernels, local(): pl.pallas_call(kernel, out_shape=(jax.ShapeDtypeStruct((PIECE, W), BF16),...  50.8 us
    unnamed x4, local copies, waits for them, and re-layouts  1.91 us

profile of v4, /device:TPU:1, one launch (start us, length us, event | category | flops | bytes accessed | tf_op | source)
XLA Modules:
  0.0 54.0 jit_solution(3402333742755506421)
XLA Ops:
  1.3 0.0 copy-start
  1.3 0.6 %copy-done = s32[1,8,1]{1,2,0:T(1,128)S(1)} copy-done((s32[1,8,1]{1,2,0:T(1,128)S(1)}, s32[1,8,1]{1,2,0:T(1,128)}, u32[]{:S(2)}) %copy-start) | copy-done | bytes 56
  1.9 50.8 %solve.1 = (bf16[32,1024]{1,0:T(8,128)(2,1)S(1)}, bf16[32,1024]{1,0:T(8,128)(2,1)S(1)}) custom-call(bf16[32,1024]{1,0:T(8,128)(2,1)} %bitcast.11, bf16[1024,1024]{1,0:T(8,128)(2,1)} %bitcast.9, bf16[8,32,1024]{2,1,0:T(8,128)(2,1)} %bitcast.10, s32[8]{0:T(128)S(1)} %bitcast.8, s32[1]{0:T(128)S(6)} %copy.9.wid_h), custom_call_target="tpu_custom_call" | custom-call | tf_op jit(solution)/shard_map/solve/pallas_call | solution.py:491
  52.7 0.6 %copy.10 = bf16[1,32,1024]{2,1,0:T(8,128)(2,1)} copy(bf16[1,32,1024]{2,1,0:T(8,128)(2,1)S(1)} %bitcast.7) | data formatting | bytes 131072
  53.3 0.6 %copy.11 = bf16[1,32,1024]{2,1,0:T(8,128)(2,1)} copy(bf16[1,32,1024]{2,1,0:T(8,128)(2,1)S(1)} %bitcast.6) | data formatting | bytes 131072
Async XLA Ops:
  1.3 0.7 %copy-start = (s32[1,8,1]{1,2,0:T(1,128)S(1)}, s32[1,8,1]{1,2,0:T(1,128)}, u32[]{:S(2)}) copy-start(s32[1,8,1]{1,2,0:T(1,128)} %param.8) | copy-start | bytes 100

commit v5 on v4

--- a/solution.py
+++ b/solution.py
@@ -39,12 +39,16 @@
 
     loads = [
         pltpu.make_async_copy(upd_h, upd_v, in_sem.at[0]),
-        pltpu.make_async_copy(inv_h, inv_v, in_sem.at[1]),
+        pltpu.make_async_copy(inv_h.at[pl.ds(0, 256)], inv_v.at[pl.ds(0, 256)], in_sem.at[1]),
         pltpu.make_async_copy(rhs_h, rhs_v, in_sem.at[2]),
         pltpu.make_async_copy(tgt_h, tgt_s, in_sem.at[3]),
         pltpu.make_async_copy(wid_h, wid_s, in_sem.at[4]),
     ]
-    for load in loads:
+    rest = [
+        pltpu.make_async_copy(inv_h.at[pl.ds(256 * r, 256)], inv_v.at[pl.ds(256 * r, 256)], in_sem.at[4 + r])
+        for r in (1, 2, 3)
+    ]
+    for load in (*loads[:2], *rest, *loads[2:]):
         load.start()
 
     barrier = pltpu.get_barrier_semaphore()
@@ -75,8 +79,11 @@
         return jnp.where(live(size), product(stacked, inv_v[...]), 0.0).astype(BF16)
 
     first = rows_for(leaf + 1)
-    loads[1].wait()
-    mats[jnp.where(leaf < 2, 0, 2), z, y, c] = coupling(first)
+    total = jnp.zeros((PIECE, W), F32)
+    for r, load in enumerate((loads[1], *rest)):
+        load.wait()
+        total = total + product(first[:, 256 * r : 256 * (r + 1)], inv_v[256 * r : 256 * (r + 1), :])
+    mats[jnp.where(leaf < 2, 0, 2), z, y, c] = jnp.where(live(PIECE), total, 0.0).astype(BF16)
     pl.semaphore_wait(barrier, GRID - 1 + 3)
 
     def block(j, h, i1, i2, core=c):
@@ -509,7 +516,7 @@
             pltpu.VMEM((6, PIECE, W), BF16),
             pltpu.VMEM((2, PIECE, W), F32),
             pltpu.VMEM((PIECE, W), F32),
-            dma((5,)),
+            dma((8,)),
             dma((3, 2, 6)),
             dma((3, 2, 28)),
             dma((3,)),

time: 54.1 us -> 54.1 us (level)
  no operation moved by 1% of the time
where the time goes in v5:
time: 54.1 us; the launch traced here: 54 us
  Pallas kernels  50.8 us (94%)
  local copies, waits for them, and re-layouts  1.91 us (4%)
  between operations  1.29 us (2%)
    pallas_call x1, Pallas kernels, local(): pl.pallas_call(kernel, out_shape=(jax.ShapeDtypeStruct((PIECE, W), BF16),...  50.8 us
    unnamed x4, local copies, waits for them, and re-layouts  1.91 us

profile of v5, /device:TPU:1, one launch (start us, length us, event | category | flops | bytes accessed | tf_op | source)
XLA Modules:
  0.0 54.0 jit_solution(18166919345493861650)
XLA Ops:
  1.3 0.0 copy-start
  1.3 0.6 %copy-done = s32[1,8,1]{1,2,0:T(1,128)S(1)} copy-done((s32[1,8,1]{1,2,0:T(1,128)S(1)}, s32[1,8,1]{1,2,0:T(1,128)}, u32[]{:S(2)}) %copy-start) | copy-done | bytes 56
  1.9 50.8 %solve.1 = (bf16[32,1024]{1,0:T(8,128)(2,1)S(1)}, bf16[32,1024]{1,0:T(8,128)(2,1)S(1)}) custom-call(bf16[32,1024]{1,0:T(8,128)(2,1)} %bitcast.11, bf16[1024,1024]{1,0:T(8,128)(2,1)} %bitcast.9, bf16[8,32,1024]{2,1,0:T(8,128)(2,1)} %bitcast.10, s32[8]{0:T(128)S(1)} %bitcast.8, s32[1]{0:T(128)S(6)} %copy.9.wid_h), custom_call_target="tpu_custom_call" | custom-call | tf_op jit(solution)/shard_map/solve/pallas_call | solution.py:498
  52.7 0.6 %copy.10 = bf16[1,32,1024]{2,1,0:T(8,128)(2,1)} copy(bf16[1,32,1024]{2,1,0:T(8,128)(2,1)S(1)} %bitcast.7) | data formatting | bytes 131072
  53.4 0.6 %copy.11 = bf16[1,32,1024]{2,1,0:T(8,128)(2,1)} copy(bf16[1,32,1024]{2,1,0:T(8,128)(2,1)S(1)} %bitcast.6) | data formatting | bytes 131072
Async XLA Ops:
  1.3 0.7 %copy-start = (s32[1,8,1]{1,2,0:T(1,128)S(1)}, s32[1,8,1]{1,2,0:T(1,128)}, u32[]{:S(2)}) copy-start(s32[1,8,1]{1,2,0:T(1,128)} %param.8) | copy-start | bytes 100
